TPU v7x, 256 devices: a whole 4x4x8 slice. The times are simulated.
256 devices in a mesh: dp: 32 (over z, y_hi, core), node: 8 (over x, y_lo).
Axes of the slice: x: 4, y: 4 (y_hi: 2, y_lo: 2; y = y_hi * 2 + y_lo), z: 8, core: 2. Of those that a mesh axis runs over, the one named last changes fastest.
Arguments:
- tokens: bfloat16 [65536, 8192], P(('dp', 'node')), may hold values from -12 to 12
- weight: bfloat16 [8192, 512], P(('dp', 'node')), may hold values from -0.0625 to 0.0625
- cotangent: bfloat16 [65536, 512], P(('dp', 'node')), may hold values from -24 to 24
- amax_history: float32 [3, 16], replicated, may hold values from 0.5 to 8
Outputs:
- keys: bfloat16 [65536, 512], P(('dp', 'node'))
- input_grad: bfloat16 [65536, 8192], P(('dp', 'node'))
- weight_grad: bfloat16 [8192, 512], P(('dp', 'node'))
- new_history: float32 [3, 16], replicated
All inputs are finite; a program needn't handle non-finite values.
Results may differ from a plain program's by a relative error of at most 0.0014.
Values may be sent and summed in bfloat16 or wider, within the bound.
No kernel may reach another device: no remote copies, remote signals or barrier semaphores. Data moves between devices by JAX's collectives and lax.ppermute only.
A program may use at most 128 MiB of HBM per device.

v0:
```python
import math

import jax
import jax.numpy as jnp
from jax import lax
from jax.sharding import PartitionSpec as P


def magnitude(array):
    return jnp.max(jnp.abs(array.astype(jnp.float32)))


def local(tokens, weight, cotangent, amax_history):
    dp_count = lax.axis_size("dp")
    node_count = lax.axis_size("node")
    tok_rows = tokens.shape[0]
    total_tokens = tok_rows * dp_count * node_count
    full_weight = lax.all_gather(weight, ("dp", "node"), axis=0, tiled=True)
    keys = jnp.dot(tokens, full_weight, preferred_element_type=jnp.float32).astype(jnp.bfloat16)
    input_grad = lax.dot_general(
        cotangent, full_weight, (((1,), (1,)), ((), ())), preferred_element_type=jnp.float32
    ).astype(jnp.bfloat16)
    summed = lax.psum_scatter(
        lax.dot_general(
            tokens, cotangent, (((0,), (0,)), ((), ())), preferred_element_type=jnp.float32
        ),
        ("dp", "node"),
        scatter_dimension=0,
        tiled=True,
    )
    weight_grad = (summed * (1.0 / math.sqrt(total_tokens))).astype(jnp.bfloat16)
    token_max, weight_max, grad_max = lax.pmax(
        (magnitude(tokens), magnitude(weight), magnitude(cotangent)), ("dp", "node")
    )
    amax = jnp.stack([token_max, weight_max, grad_max])
    new_history = jnp.concatenate([amax[:, None], amax_history[:, :-1]], axis=1)
    return (keys, input_grad, weight_grad, new_history)


def solution(mesh):
    return jax.shard_map(
        local,
        mesh=mesh,
        in_specs=(P(("dp", "node"), None), P(("dp", "node"), None), P(("dp", "node"), None), P()),
        out_specs=(P(("dp", "node"), None), P(("dp", "node"), None), P(("dp", "node"), None), P()),
        check_vma=False,
    )
```

profile of v0, /device:TPU:0, one launch (start us, length us, event | category | flops | bytes accessed | tf_op | source)
XLA Modules:
  0.0 2037.6 jit_solution(17557729570236395526)
XLA Ops:
  7.2 0.0 all-gather.2.cloned.1.call-start
  7.2 0.7 all-gather.2.cloned.1.call-update
  7.9 0.0 reduce-scatter.2.cloned.1.call-start
  7.9 10.3 fusion
  18.3 0.0 copy-start.2
  18.3 0.0 copy-start.1
  18.3 0.0 copy-start.3
  18.3 0.0 reduce-scatter.2.cloned.1.call-update
  18.3 0.7 copy-done.2
  19.0 0.6 abs_reduce_fusion.2
  19.6 0.0 copy-done.1
  19.6 0.6 abs_reduce_fusion.1
  20.3 3.3 abs_reduce_fusion
  23.6 79.1 %all-reduce = (f32[1]{0:T(128)}, f32[1]{0:T(128)}, f32[1]{0:T(128)}) all-reduce(f32[1]{0:T(128)} %bitcast.2, f32[1]{0:T(128)} %bitcast.1, f32[1]{0:T(128)} %bitcast), channel_id=1, replica_groups=mesh['dp'=32,'node'=8] {'dp','node'}, use_global_device_ids=true, to_apply=%region_6.0 | all-reduce | flops 3 | bytes 24 | tf_op jit(solution)/shard_map/pmax | solution.py:32
  102.7 2.0 maximum_bitcast_fusion
  104.7 0.1 copy.8
  104.8 0.0 copy-done.3
  104.8 0.7 pad_maximum_fusion
  105.4 623.8 %all-gather.2.cloned.1.call-done = bf16[8192,512]{1,0:T(8,128)(2,1)} async-done(((bf16[32,512]{1,0:T(8,128)(2,1)}), bf16[8192,512]{1,0:T(8,128)(2,1)}) %all-gather.2.cloned.1.call-update) | async-done | bytes 8388624 | tf_op jit(solution)/shard_map/all_gather | solution.py:18
  729.3 0.0 copy-start
  729.3 0.0 copy-start.4
  729.3 7.9 convolution_convert_fusion
  737.2 0.0 copy-done
  737.2 0.0 copy-done.4
  737.2 3.0 convolution_convert_fusion.1
  740.2 1289.1 %reduce-scatter.2.cloned.1.call-done = f32[32,512]{1,0:T(8,128)} async-done(((f32[8192,512]{1,0:T(8,128)}), f32[32,512]{1,0:T(8,128)}) %reduce-scatter.2.cloned.1.call-update) | async-done | bytes 65552 | tf_op jit(solution)/shard_map/reduce_scatter | solution.py:23
  2029.3 1.5 multiply_convert_fusion
Async XLA Ops:
  7.2 722.1 %all-gather.2.cloned.1.call-start = ((), (), s32[]{:S(2)}) async-start(), calls=%async_computation.1 | async-start | bytes 8421376 | tf_op jit(solution)/shard_map/all_gather | solution.py:18
  7.9 2021.4 %reduce-scatter.2.cloned.1.call-start = ((), (), s32[]{:S(2)}) async-start(), calls=%async_computation.2 | async-start | bytes 16842752 | tf_op jit(solution)/shard_map/reduce_scatter | solution.py:23
  18.3 0.8 copy-start.2
  18.3 1.4 copy-start.1
  18.3 86.5 %copy-start.3 = (f32[3,16]{1,0:T(4,128)S(1)}, f32[3,16]{1,0:T(4,128)}, u32[]{:S(2)}) copy-start(f32[3,16]{1,0:T(4,128)} %param.7) | copy-start | bytes 580
  729.3 7.9 copy-start
  729.3 7.9 copy-start.4
Sparse Core Ops, SparseCore 0:
  9.9 719.3 all-gather.1
  731.8 1297.5 reduce-scatter.1
where the time goes:
time: 2040 us
  waiting for transfers between devices  1910 us (94%)
  blocking collectives  79.1 us (4%)
  matrix products  21.3 us (1%)
    reduce_scatter x1, waiting for transfers between devices, local(): lax.psum_scatter(lax.dot_general(tokens, cotangent, (((0,), (0,)), ((), (...  1290 us
    all_gather x1, waiting for transfers between devices, local(): full_weight = lax.all_gather(weight, ('dp', 'node'), axis=0, tiled=True)  624 us
    pmax x1, blocking collectives, local(): lax.pmax((magnitude(tokens), magnitude(weight), magnitude(cotangent)), ('...  79.1 us
  transfers between devices with their start and end apart: 2, of which 2 were waited for; matrix products, arithmetic and copies ran while one was open for 1% of the time, Pallas kernels for 0%

commit v1 on v0

v1 whole, which is shorter than its diff:
```python
import jax
import jax.numpy as jnp
from jax import lax
from jax.experimental import pallas as pl
from jax.experimental.pallas import tpu as pltpu
from jax.sharding import Mesh, PartitionSpec as P

AXES = ("z", "yh", "core", "x", "yl")
SIZES = (8, 2, 2, 4, 2)
PLANE = ("yh", "x", "yl")
ROWS = 256
KV = 512
HALF = 4096
CHUNK = 256
NOTE = 128
SENT = HALF + KV + NOTE
BOTH = 2 * ROWS
BF16, F32 = jnp.bfloat16, jnp.float32
VMEM_LIMIT = 48 * 1024 * 1024


def dot(a, b, contract):
    return lax.dot_general(a, b, ((contract[:1], contract[1:]), ((), ())), preferred_element_type=F32)


def top(a):
    a = jnp.abs(a)
    while a.shape[0] > 16:
        half = a.shape[0] // 2
        a = jnp.maximum(a[:half], a[half:])
    return jnp.max(jnp.max(a.astype(F32), axis=1, keepdims=True), axis=0, keepdims=True)


def normalise(m):
    x, k, s = m * 2.0**-24, jnp.full_like(m, -24.0), jnp.full_like(m, 2.0**-24)
    for b in (64, 32, 16, 8, 4, 2, 1):
        low = x < 2.0**-b
        x, k, s = jnp.where(low, x * 2.0**b, x), jnp.where(low, k + b, k), jnp.where(low, s * 2.0**b, s)
    return s, k


def bound_of(token_max, grad_max):
    return token_max * grad_max * float(BOTH)


def encode8(x):
    x2 = x * x
    x4 = x2 * x2
    return (x4 * x2) * (jnp.abs(x) * x)


def encode16(x):
    x2 = x * x
    x4 = x2 * x2
    x8 = x4 * x4
    return (x8 * x4) * (x2 * jnp.abs(x) * x)


def decode(y, power, shift):
    a = jnp.abs(y)
    v = jnp.where(a > 0.0, jnp.exp2(jnp.log2(a) * (1.0 / power) - shift), 0.0)
    return jnp.where(y < 0.0, -v, v)


def note(values, shape):
    rows = lax.broadcasted_iota(jnp.int32, shape, len(shape) - 2)
    out = jnp.zeros(shape, F32)
    for i, v in enumerate(values):
        out = jnp.where(rows == i, v, out)
    return out.astype(BF16)


def pack_kernel(core, tokens, cot, weight, sent, best):
    i = pl.program_id(0)
    other = pl.multiple_of((1 - core[0]) * CHUNK, CHUNK)
    width = tokens.shape[1] // (2 * CHUNK)
    for j in range(width):
        at = pl.multiple_of(i * (width * CHUNK) + j * CHUNK, CHUNK)
        sent[:, pl.ds(at, CHUNK)] = tokens[:, pl.ds(2 * CHUNK * j + other, CHUNK)]
    m = top(tokens[...])

    @pl.when(i == 0)
    def _():
        best[...] = jnp.zeros_like(best)

    best[...] = jnp.maximum(best[...], m)

    @pl.when(i == pl.num_programs(0) - 1)
    def _():
        sent[:, HALF:HALF + KV] = cot[...]
        sent[:, HALF + KV:] = note([best[:1, :1], top(weight[...]), top(cot[...])], (ROWS, NOTE))


def pack(core, tokens, cot, weight):
    steps = 4
    return pl.pallas_call(
        pack_kernel,
        out_shape=jax.ShapeDtypeStruct((ROWS, SENT), BF16),
        grid_spec=pltpu.PrefetchScalarGridSpec(
            num_scalar_prefetch=1,
            grid=(steps,),
            in_specs=[
                pl.BlockSpec((ROWS, 2 * HALF // steps), lambda i, c: (0, i)),
                pl.BlockSpec((ROWS, KV), lambda i, c: (0, 0)),
                pl.BlockSpec((32, KV), lambda i, c: (0, 0)),
            ],
            out_specs=pl.BlockSpec((ROWS, SENT), lambda i, c: (0, 0)),
            scratch_shapes=[pltpu.VMEM((8, 128), F32)],
        ),
        compiler_params=pltpu.CompilerParams(vmem_limit_bytes=VMEM_LIMIT),
        cost_estimate=pl.CostEstimate(flops=8_000_000, bytes_accessed=7_000_000, transcendentals=0),
        name="pack",
    )(core, tokens, cot, weight)


def grad_kernel(core, tokens, cot, own_note, got, got_cot, got_note, out):
    i = pl.program_id(0)
    own = pl.multiple_of(core[0] * CHUNK, CHUNK)
    notes = jnp.maximum(own_note[...].astype(F32), got_note[...].astype(F32))
    maxima = [notes[r:r + 1, 0:1] for r in range(3)]
    scale, k = normalise(maxima[0] * maxima[2] * float(2 * ROWS))
    scale = scale * 2.0**15
    pieces = got.shape[1] // CHUNK
    for j in range(pieces):
        mine = tokens[:, pl.ds(2 * CHUNK * j + own, CHUNK)]
        p = dot(mine, cot[...], (0, 0)) + dot(got[:, CHUNK * j:CHUNK * (j + 1)], got_cot[...], (0, 0))
        y = encode8(p * scale).astype(BF16)
        at = (i * (pieces // 2) + j // 2) * 2 * KV
        for d in range(8):
            for h in range(2):
                row = d * 32 + h * 16
                out[(j % 2) * 8 + d, :, pl.ds(pl.multiple_of(at + h * KV, KV), KV)] = y[row:row + 16, :]

    @pl.when(i == 0)
    def _():
        out[:, :, 2 * HALF:] = note(maxima + [k], (16, 16, NOTE))


def grad(core, tokens, cot, sent, got):
    steps = 4
    return pl.pallas_call(
        grad_kernel,
        out_shape=jax.ShapeDtypeStruct((16, 16, 2 * HALF + NOTE), BF16),
        grid_spec=pltpu.PrefetchScalarGridSpec(
            num_scalar_prefetch=1,
            grid=(steps,),
            in_specs=[
                pl.BlockSpec((ROWS, 2 * HALF // steps), lambda i, c: (0, i)),
                pl.BlockSpec((ROWS, KV), lambda i, c: (0, 0)),
                pl.BlockSpec((16, NOTE), lambda i, c: (0, (HALF + KV) // NOTE)),
                pl.BlockSpec((ROWS, HALF // steps), lambda i, c: (0, i)),
                pl.BlockSpec((ROWS, KV), lambda i, c: (0, HALF // KV)),
                pl.BlockSpec((16, NOTE), lambda i, c: (0, (HALF + KV) // NOTE)),
            ],
            out_specs=pl.BlockSpec((16, 16, 2 * HALF + NOTE), lambda i, c: (0, 0, 0)),
        ),
        compiler_params=pltpu.CompilerParams(vmem_limit_bytes=VMEM_LIMIT),
        cost_estimate=pl.CostEstimate(flops=2_200_000_000, bytes_accessed=11_000_000, transcendentals=0),
        name="grad",
    )(core, tokens, cot, sent, got, got, got)


def plane_kernel(parts, notes, out):
    maxima = [jnp.max(notes[:, r, :].astype(F32), axis=0, keepdims=True)[:, 0:1] for r in range(3)]
    width = 2 * KV
    for j in range(parts.shape[2] // width):
        total = jnp.zeros((16, width), F32)
        for s in range(16):
            shift = notes[s, 3:4, 0:1].astype(F32) + 15.0
            total += decode(parts[s, :, j * width:(j + 1) * width].astype(F32), 8, shift)
        scale, k = normalise(top(total))
        out[j, :, :width] = encode16(total * (scale * 2.0**7)).astype(BF16)
        out[j, :, width:] = note(maxima + [k], (16, NOTE))


def plane(parts):
    steps = 4
    return pl.pallas_call(
        plane_kernel,
        out_shape=jax.ShapeDtypeStruct((8, 16, 2 * KV + NOTE), BF16),
        grid=(steps,),
        in_specs=[
            pl.BlockSpec((16, 16, 2 * HALF // steps), lambda i: (0, 0, i)),
            pl.BlockSpec((16, 16, NOTE), lambda i: (0, 0, 2 * HALF // NOTE)),
        ],
        out_specs=pl.BlockSpec((8 // steps, 16, 2 * KV + NOTE), lambda i: (i, 0, 0)),
        compiler_params=pltpu.CompilerParams(vmem_limit_bytes=VMEM_LIMIT),
        cost_estimate=pl.CostEstimate(flops=20_000_000, bytes_accessed=5_000_000, transcendentals=4_000_000),
        name="plane",
    )(parts, parts)


def last_kernel(parts, history, weight_grad, new_history):
    total = jnp.zeros((16, 2 * KV), F32)
    for s in range(8):
        shift = parts[s, 3:4, 2 * KV:2 * KV + 1].astype(F32) + 7.0
        total += decode(parts[s, :, :2 * KV].astype(F32), 16, shift)
    total = (total * (1.0 / 256.0)).astype(BF16)
    weight_grad[:16, :] = total[:, :KV]
    weight_grad[16:, :] = total[:, KV:]
    notes = jnp.max(parts[:, :, 2 * KV:].astype(F32), axis=0)
    new_history[...] = jnp.concatenate([notes[:3, :1], history[:, :15]], axis=1)


def last(parts, history):
    return pl.pallas_call(
        last_kernel,
        out_shape=(jax.ShapeDtypeStruct((32, KV), BF16), jax.ShapeDtypeStruct((3, 16), F32)),
        compiler_params=pltpu.CompilerParams(vmem_limit_bytes=VMEM_LIMIT),
        cost_estimate=pl.CostEstimate(flops=1_000_000, bytes_accessed=330_000, transcendentals=260_000),
        name="last",
    )(parts, history)


def theirs_kernel(tokens, cot, weight, input_grad, keys):
    i = pl.program_id(0)
    w = weight[...]
    p = dot(tokens[...], w, (1, 0))

    @pl.when(i == 0)
    def _():
        keys[...] = p

    @pl.when(i > 0)
    def _():
        keys[...] += p

    input_grad[...] = dot(cot[...], w, (1, 1)).astype(BF16)


def theirs(got, weight):
    steps = 4
    return pl.pallas_call(
        theirs_kernel,
        out_shape=(jax.ShapeDtypeStruct((ROWS, HALF), BF16), jax.ShapeDtypeStruct((ROWS, KV), F32)),
        grid=(steps,),
        in_specs=[
            pl.BlockSpec((ROWS, HALF // steps), lambda i: (0, i)),
            pl.BlockSpec((ROWS, KV), lambda i: (0, HALF // KV)),
            pl.BlockSpec((HALF // steps, KV), lambda i: (i, 0)),
        ],
        out_specs=(
            pl.BlockSpec((ROWS, HALF // steps), lambda i: (0, i)),
            pl.BlockSpec((ROWS, KV), lambda i: (0, 0)),
        ),
        compiler_params=pltpu.CompilerParams(vmem_limit_bytes=VMEM_LIMIT),
        cost_estimate=pl.CostEstimate(flops=2_200_000_000, bytes_accessed=9_000_000, transcendentals=0),
        name="theirs",
    )(got, got, weight)


def ours_kernel(core, tokens, cot, weight, input_grad, keys):
    i = pl.program_id(0)
    own = pl.multiple_of(core[0] * CHUNK, CHUNK)
    total = jnp.zeros((ROWS, KV), F32)
    for j in range(weight.shape[0] // CHUNK):
        w = weight[j * CHUNK:(j + 1) * CHUNK, :]
        total += dot(tokens[:, pl.ds(2 * CHUNK * j + own, CHUNK)], w, (1, 0))
        input_grad[:, pl.ds(2 * CHUNK * j + own, CHUNK)] = dot(cot[...], w, (1, 1)).astype(BF16)

    @pl.when(i == 0)
    def _():
        keys[...] = total

    @pl.when(i > 0)
    def _():
        keys[...] += total


def ours(core, tokens, cot, weight):
    steps = 4
    return pl.pallas_call(
        ours_kernel,
        out_shape=(jax.ShapeDtypeStruct((ROWS, 2 * HALF), BF16), jax.ShapeDtypeStruct((ROWS, KV), F32)),
        grid_spec=pltpu.PrefetchScalarGridSpec(
            num_scalar_prefetch=1,
            grid=(steps,),
            in_specs=[
                pl.BlockSpec((ROWS, 2 * HALF // steps), lambda i, c: (0, i)),
                pl.BlockSpec((ROWS, KV), lambda i, c: (0, 0)),
                pl.BlockSpec((HALF // steps, KV), lambda i, c: (i, 0)),
            ],
            out_specs=(
                pl.BlockSpec((ROWS, 2 * HALF // steps), lambda i, c: (0, i)),
                pl.BlockSpec((ROWS, KV), lambda i, c: (0, 0)),
            ),
        ),
        compiler_params=pltpu.CompilerParams(vmem_limit_bytes=VMEM_LIMIT),
        cost_estimate=pl.CostEstimate(flops=2_200_000_000, bytes_accessed=12_000_000, transcendentals=0),
        name="ours",
    )(core, tokens, cot, weight)


def join_kernel(core, columns, ours_keys, got_keys, _, input_grad, keys, sem):
    other = pl.multiple_of((1 - core[0]) * CHUNK, CHUNK)
    copies = [
        pltpu.make_async_copy(
            columns.at[:, pl.ds(j * CHUNK, CHUNK)],
            input_grad.at[:, pl.ds(2 * CHUNK * j + other, CHUNK)],
            sem.at[j],
        )
        for j in range(HALF // CHUNK)
    ]
    for c in copies:
        c.start()
    keys[...] = (ours_keys[...] + got_keys[...]).astype(BF16)
    for c in copies:
        c.wait()


def join(core, columns, ours_keys, got_keys, input_grad):
    return pl.pallas_call(
        join_kernel,
        out_shape=(jax.ShapeDtypeStruct((ROWS, 2 * HALF), BF16), jax.ShapeDtypeStruct((ROWS, KV), BF16)),
        in_specs=[
            pl.BlockSpec(memory_space=pltpu.SMEM),
            pl.BlockSpec(memory_space=pl.ANY),
            pl.BlockSpec(memory_space=pltpu.VMEM),
            pl.BlockSpec(memory_space=pltpu.VMEM),
            pl.BlockSpec(memory_space=pl.ANY),
        ],
        out_specs=(pl.BlockSpec(memory_space=pl.ANY), pl.BlockSpec(memory_space=pltpu.VMEM)),
        scratch_shapes=[pltpu.SemaphoreType.DMA((HALF // CHUNK,))],
        input_output_aliases={4: 0},
        compiler_params=pltpu.CompilerParams(vmem_limit_bytes=VMEM_LIMIT),
        cost_estimate=pl.CostEstimate(flops=130_000, bytes_accessed=5_400_000, transcendentals=0),
        name="join",
    )(core, columns, ours_keys, got_keys, input_grad)


SWAP = [(0, 1), (1, 0)]


def local(tokens, weight, cot, history):
    core = lax.axis_index("core").astype(jnp.int32).reshape(1)
    sent = pack(core, tokens, cot, weight)
    got = lax.ppermute(sent, "core", SWAP)
    near = lax.all_to_all(jnp.broadcast_to(weight[None], (16, 32, KV)), PLANE, 0, 0, tiled=True)
    half_weight = lax.all_gather(near.reshape(512, KV), "z", axis=0, tiled=True)
    coded = grad(core, tokens, cot, sent, got)
    parts = lax.all_to_all(coded, PLANE, 0, 0, tiled=True)
    parts = lax.all_to_all(plane(parts), "z", 0, 0, tiled=True)
    weight_grad, new_history = last(parts, history)
    columns, their_keys = theirs(got, half_weight)
    columns = lax.ppermute(columns, "core", SWAP)
    got_keys = lax.ppermute(their_keys, "core", SWAP)
    input_grad, our_keys = ours(core, tokens, cot, half_weight)
    input_grad, keys = join(core, columns, our_keys, got_keys, input_grad)
    return (keys, input_grad, weight_grad, new_history)


def solution(mesh):
    split = Mesh(mesh.devices.reshape(SIZES), AXES)
    rows = P(AXES, None)
    return jax.shard_map(
        local,
        mesh=split,
        in_specs=(rows, rows, rows, P()),
        out_specs=(rows, rows, rows, P()),
        check_vma=False,
    )
```

time: 2040 us -> 156 us (0.08)
  waiting for transfers between devices: 1910 us -> 71.1 us
  blocking collectives: 79.1 us -> 16.7 us
  Pallas kernels: 0 us -> 33.6 us
  matrix products: 21.3 us -> 0 us
    reduce_scatter x1 -> x0, waiting for transfers between devices: 1290 us -> none  [local(): lax.psum_scatter(lax.dot_general(tokens, cotangent, (((0,), (0,)), ((), (...]
    all_gather x1, waiting for transfers between devices: 624 us -> 32.4 us  [local(): half_weight = lax.all_gather(near.reshape(512, KV), 'z', axis=0, tiled=True)]
    pmax x1 -> x0, blocking collectives: 79.1 us -> none  [local(): lax.pmax((magnitude(tokens), magnitude(weight), magnitude(cotangent)), ('...]
    all_to_all x0 -> x2, waiting for transfers between devices: none -> 34.1 us  [the longest x1 22 us: local(): parts = lax.all_to_all(coded, PLANE, 0, 0, tiled=True)]
    pallas_call x0 -> x7, Pallas kernels: none -> 33.6 us  [the longest x1 7.54 us: grad(): pl.pallas_call(grad_kernel, out_shape=jax.ShapeDtypeStruct((16, 16, 2 * H...]
    dot_general x3 -> x0, matrix products: 21.3 us -> none  [the longest x1 10.3 us: local(): lax.dot_general(tokens, cotangent, (((0,), (0,)), ((), ())), preferred_el...]
  transfers between devices with their start and end apart: 2 -> 6, of which waited for: 2 -> 4; matrix products, arithmetic and copies ran while one was open for 1% -> 0% of each run, Pallas kernels for 0% -> 20%
where the time goes in v1:
time: 156 us; the launch traced here: 154 us
  waiting for transfers between devices  71.1 us (46%)
  Pallas kernels  33.6 us (22%)
  blocking collectives  16.7 us (11%)
  between operations  14.1 us (9%)
  starting transfers between devices  12.8 us (8%)
  local copies, waits for them, and re-layouts  5.49 us (4%)
    all_gather x1, waiting for transfers between devices, local(): half_weight = lax.all_gather(near.reshape(512, KV), 'z', axis=0, tiled=True)  32.4 us
    all_to_all x1, waiting for transfers between devices, local(): parts = lax.all_to_all(coded, PLANE, 0, 0, tiled=True)  22 us
    all_to_all x1, blocking collectives, local(): lax.all_to_all(jnp.broadcast_to(weight[None], (16, 32, KV)), PLANE, 0, 0,...  16.7 us
    all_to_all x1, waiting for transfers between devices, local(): parts = lax.all_to_all(plane(parts), 'z', 0, 0, tiled=True)  12.1 us
    all_to_all x1, starting transfers between devices, local(): parts = lax.all_to_all(plane(parts), 'z', 0, 0, tiled=True)  8.17 us
    pallas_call x1, Pallas kernels, grad(): pl.pallas_call(grad_kernel, out_shape=jax.ShapeDtypeStruct((16, 16, 2 * H...  7.54 us
    pallas_call x1, Pallas kernels, plane(): pl.pallas_call(plane_kernel, out_shape=jax.ShapeDtypeStruct((8, 16, 2 * K...  6.71 us
    pallas_call x1, Pallas kernels, theirs(): pl.pallas_call(theirs_kernel, out_shape=(jax.ShapeDtypeStruct((ROWS, HALF...  6.52 us
  transfers between devices with their start and end apart: 6, of which 4 were waited for; matrix products, arithmetic and copies ran while one was open for 0% of the time, Pallas kernels for 20%

profile of v1, /device:TPU:0, one launch (start us, length us, event | category | flops | bytes accessed | tf_op | source)
XLA Modules:
  0.0 153.8 jit_solution(12981653444708731956)
XLA Ops:
  7.2 0.0 all-gather.2.cloned.1.call-start
  7.2 0.8 broadcast_in_dim.2
  8.0 16.7 %all_to_all.15 = bf16[16,32,512]{2,1,0:T(8,128)(2,1)} all-to-all(bf16[16,32,512]{2,1,0:T(8,128)(2,1)S(1)} %broadcast_in_dim.2), channel_id=1, replica_groups=mesh['z'=8,'yh'=2,'core'=2,'x'=4,'yl'=2] {'yh','x','yl'}, dimensions={0} | all-to-all | bytes 1048576 | tf_op jit(solution)/shard_map/all_to_all | solution.py:338
  24.7 0.0 all-gather.2.cloned.1.call-update
  24.7 0.0 copy-start.1
  24.8 0.9 copy-done.1
  25.7 0.0 copy-start.3
  25.7 0.8 copy-done.3
  26.5 3.5 %pack.1.own_note = bf16[256,4736]{1,0:T(8,128)(2,1)S(1)} custom-call(s32[1]{0:T(128)} %bitcast.core, bf16[256,8192]{1,0:T(8,128)(2,1)} %tokens.5, bf16[256,512]{1,0:T(8,128)(2,1)S(1)} %copy-done.1, bf16[32,512]{1,0:T(8,128)(2,1)S(1)} %copy-done.3), custom_call_target="tpu_custom_call" | custom-call | flops 8000000 | bytes 7000000 | tf_op jit(solution)/shard_map/pack/pallas_call | solution.py:96
  29.9 0.1 collective-permute-start
  30.0 4.6 %collective-permute-done.tokens.cot.got.got_cot.got_note = bf16[256,4736]{1,0:T(8,128)(2,1)S(1)} collective-permute-done((bf16[256,4736]{1,0:T(8,128)(2,1)S(1)}, bf16[256,4736]{1,0:T(8,128)(2,1)S(1)}, u32[]{:S(2)}, u32[]{:S(2)}) %collective-permute-start) | collective-permute-done | bytes 2424864 | tf_op jit(solution)/shard_map/ppermute | solution.py:337
  34.6 7.5 %grad.1 = bf16[16,16,8320]{2,1,0:T(8,128)(2,1)} custom-call(s32[1]{0:T(128)} %bitcast.core, bf16[256,8192]{1,0:T(8,128)(2,1)} %tokens.5, bf16[256,512]{1,0:T(8,128)(2,1)S(1)} %copy-done.1, bf16[256,4736]{1,0:T(8,128)(2,1)S(1)} %pack.1.own_note, bf16[256,4736]{1,0:T(8,128)(2,1)S(1)} %collective-permute-done.tokens.cot.got.got_cot.got_note, ...), custom_call_target="tpu_custom_call" | custom-call | flops 2200000000 | bytes 11000000 | tf_op jit(solution)/shard_map/grad/pallas_call | solution.py:141
  42.2 4.5 %all-to-all-start.1 = ((bf16[16,16,8320]{2,1,0:T(8,128)(2,1)}), bf16[16,16,8320]{2,1,0:T(8,128)(2,1)}, u32[]{:S(2)}, u32[]{:S(2)}) async-start(bf16[16,16,8320]{2,1,0:T(8,128)(2,1)} %grad.1), calls=%async_computation.1 | async-start | bytes 8519680 | tf_op jit(solution)/shard_map/all_to_all | solution.py:341
  46.7 32.4 %all-gather.2.cloned.1.call-done.weight = bf16[4096,512]{1,0:T(8,128)(2,1)} async-done(((bf16[512,512]{1,0:T(8,128)(2,1)}), bf16[4096,512]{1,0:T(8,128)(2,1)}) %all-gather.2.cloned.1.call-update) | async-done | bytes 4194320 | tf_op jit(solution)/shard_map/all_gather | solution.py:339
  79.1 6.5 %theirs.1 = (bf16[256,4096]{1,0:T(8,128)(2,1)}, f32[256,512]{1,0:T(8,128)S(1)}) custom-call(bf16[256,4736]{1,0:T(8,128)(2,1)S(1)} %collective-permute-done.tokens.cot.got.got_cot.got_note, bf16[256,4736]{1,0:T(8,128)(2,1)S(1)} %collective-permute-done.tokens.cot.got.got_cot.got_note, bf16[4096,512]{1,0:T(8,128)(2,1)} %all-gather.2.cloned.1.call-done.weight), custom_call_target="tpu_custom_call" | custom-call | flops 2200000000 | bytes 9000000 | tf_op jit(solution)/shard_map/theirs/pallas_call | solution.py:233
  85.6 0.0 copy-start.4
  85.6 0.8 copy-done.4
  86.4 0.0 copy-start.5
  86.4 0.0 copy-start.2
  86.4 0.0 collective-permute-start.1
  86.4 22.0 %all-to-all-done.1.parts.notes = bf16[16,16,8320]{2,1,0:T(8,128)(2,1)} async-done(((bf16[16,16,8320]{2,1,0:T(8,128)(2,1)}), bf16[16,16,8320]{2,1,0:T(8,128)(2,1)}, u32[]{:S(2)}, u32[]{:S(2)}) %all-to-all-start.1) | async-done | bytes 4259872 | tf_op jit(solution)/shard_map/all_to_all | solution.py:341
  108.4 6.7 %plane.1 = bf16[8,16,1152]{2,1,0:T(8,128)(2,1)} custom-call(bf16[16,16,8320]{2,1,0:T(8,128)(2,1)} %all-to-all-done.1.parts.notes, bf16[16,16,8320]{2,1,0:T(8,128)(2,1)} %all-to-all-done.1.parts.notes), custom_call_target="tpu_custom_call" | custom-call | flops 20000000 | bytes 5000000 | tf_op jit(solution)/shard_map/plane/pallas_call | solution.py:178
  115.1 8.2 %all-to-all-start.2 = ((bf16[8,16,1152]{2,1,0:T(8,128)(2,1)}), bf16[8,16,1152]{2,1,0:T(8,128)(2,1)S(1)}, u32[]{:S(2)}, u32[]{:S(2)}) async-start(bf16[8,16,1152]{2,1,0:T(8,128)(2,1)} %plane.1), calls=%async_computation.2 | async-start | bytes 589824 | tf_op jit(solution)/shard_map/all_to_all | solution.py:342
  123.3 0.0 collective-permute-start.2
  123.3 12.1 %all-to-all-done.2.parts = bf16[8,16,1152]{2,1,0:T(8,128)(2,1)S(1)} async-done(((bf16[8,16,1152]{2,1,0:T(8,128)(2,1)}), bf16[8,16,1152]{2,1,0:T(8,128)(2,1)S(1)}, u32[]{:S(2)}, u32[]{:S(2)}) %all-to-all-start.2) | async-done | bytes 294944 | tf_op jit(solution)/shard_map/all_to_all | solution.py:342
  135.4 0.0 copy-done.5
  135.4 0.9 last.1
  136.3 0.0 copy-done.2
  136.3 0.0 copy-start
  136.3 2.2 %copy-done = bf16[256,8192]{1,0:T(8,128)(2,1)S(1)} copy-done((bf16[256,8192]{1,0:T(8,128)(2,1)S(1)}, bf16[256,8192]{1,0:T(8,128)(2,1)}, u32[]{:S(2)}) %copy-start) | copy-done | bytes 4194328
  138.5 6.3 %ours.1 = (bf16[256,8192]{1,0:T(8,128)(2,1)}, f32[256,512]{1,0:T(8,128)S(1)}) custom-call(s32[1]{0:T(128)} %bitcast.core, bf16[256,8192]{1,0:T(8,128)(2,1)S(1)} %copy-done, bf16[256,512]{1,0:T(8,128)(2,1)S(1)} %copy-done.2, bf16[4096,512]{1,0:T(8,128)(2,1)} %all-gather.2.cloned.1.call-done.weight), custom_call_target="tpu_custom_call" | custom-call | flops 2200000000 | bytes 12000000 | tf_op jit(solution)/shard_map/ours/pallas_call | solution.py:272
  144.8 0.0 collective-permute-done.2.got_keys
  144.8 0.0 collective-permute-done.1.columns
  144.8 2.1 %join.1 = (bf16[256,8192]{1,0:T(8,128)(2,1)}, bf16[256,512]{1,0:T(8,128)(2,1)}) custom-call(s32[1]{0:T(128)} %bitcast.core, bf16[256,4096]{1,0:T(8,128)(2,1)S(1)} %collective-permute-done.1.columns, f32[256,512]{1,0:T(8,128)S(1)} %get-tuple-element.13.ours_keys, f32[256,512]{1,0:T(8,128)S(1)} %collective-permute-done.2.got_keys, ...), custom_call_target="tpu_custom_call", output_to_operand_aliasing={{0}: (4, {})} | custom-call | flops 130000 | bytes 5400000 | tf_op jit(solution)/shard_map/join/pallas_call | solution.py:312
Async XLA Ops:
  7.2 71.9 %all-gather.2.cloned.1.call-start = ((), (), s32[]{:S(2)}) async-start(), calls=%async_computation.3 | async-start | bytes 4718592 | tf_op jit(solution)/shard_map/all_gather | solution.py:339
  24.7 1.0 copy-start.1
  25.7 0.8 copy-start.3
  29.9 4.7 %collective-permute-start = (bf16[256,4736]{1,0:T(8,128)(2,1)S(1)}, bf16[256,4736]{1,0:T(8,128)(2,1)S(1)}, u32[]{:S(2)}, u32[]{:S(2)}) collective-permute-start(bf16[256,4736]{1,0:T(8,128)(2,1)S(1)} %pack.1.own_note), channel_id=1, source_target_pairs={{0,8},{8,0},{1,9},{9,1},{2,10},{10,2},{3,11},{11,3},{4,12},{12,4},... | collective-permute-start | bytes 7274504 | tf_op jit(solution)/shard_map/ppermute | solution.py:337
  42.2 66.2 %all-to-all-start.1 = ((bf16[16,16,8320]{2,1,0:T(8,128)(2,1)}), bf16[16,16,8320]{2,1,0:T(8,128)(2,1)}, u32[]{:S(2)}, u32[]{:S(2)}) async-start(bf16[16,16,8320]{2,1,0:T(8,128)(2,1)} %grad.1), calls=%async_computation.1 | async-start | bytes 8519680 | tf_op jit(solution)/shard_map/all_to_all | solution.py:341
  85.6 0.8 copy-start.4
  86.4 49.0 %copy-start.5 = (f32[3,16]{1,0:T(4,128)S(1)}, f32[3,16]{1,0:T(4,128)}, u32[]{:S(2)}) copy-start(f32[3,16]{1,0:T(4,128)} %history.1) | copy-start | bytes 580
  86.4 49.9 %copy-start.2 = (bf16[256,512]{1,0:T(8,128)(2,1)S(1)}, bf16[256,512]{1,0:T(8,128)(2,1)}, u32[]{:S(2)}) copy-start(bf16[256,512]{1,0:T(8,128)(2,1)} %cot.5) | copy-start | bytes 786436
  86.4 58.4 %collective-permute-start.1 = (bf16[256,4096]{1,0:T(8,128)(2,1)}, bf16[256,4096]{1,0:T(8,128)(2,1)S(1)}, u32[]{:S(2)}, u32[]{:S(2)}) collective-permute-start(bf16[256,4096]{1,0:T(8,128)(2,1)} %get-tuple-element.12), channel_id=1, source_target_pairs={{0,8},{8,0},{1,9},{9,1},{2,10},{10,2},{3,11},{11,3},{4,12},{12,4},... | collective-permute-start | bytes 6291464 | tf_op jit(solution)/shard_map/ppermute | solution.py:345
  115.1 20.3 %all-to-all-start.2 = ((bf16[8,16,1152]{2,1,0:T(8,128)(2,1)}), bf16[8,16,1152]{2,1,0:T(8,128)(2,1)S(1)}, u32[]{:S(2)}, u32[]{:S(2)}) async-start(bf16[8,16,1152]{2,1,0:T(8,128)(2,1)} %plane.1), calls=%async_computation.2 | async-start | bytes 589824 | tf_op jit(solution)/shard_map/all_to_all | solution.py:342
  123.3 21.5 %collective-permute-start.2 = (f32[256,512]{1,0:T(8,128)}, f32[256,512]{1,0:T(8,128)S(1)}, u32[]{:S(2)}, u32[]{:S(2)}) collective-permute-start(f32[256,512]{1,0:T(8,128)} %copy-done.4), channel_id=1, source_target_pairs={{0,8},{8,0},{1,9},{9,1},{2,10},{10,2},{3,11},{11,3},{4,12},{12,4},... | collective-permute-start | bytes 1572872 | tf_op jit(solution)/shard_map/ppermute | solution.py:346
  136.3 2.2 %copy-start = (bf16[256,8192]{1,0:T(8,128)(2,1)S(1)}, bf16[256,8192]{1,0:T(8,128)(2,1)}, u32[]{:S(2)}) copy-start(bf16[256,8192]{1,0:T(8,128)(2,1)} %tokens.5) | copy-start | bytes 12582916
Sparse Core Ops, SparseCore 0:
  24.9 54.1 all-gather.1
